TPU v7x, 512 devices: a whole 4x8x8 slice. The times are simulated.
512 devices in a mesh: label: 64 (over y, x, core), query: 8 (over z).
Axes of the slice: x: 4, y: 8, z: 8, core: 2. Of those that a mesh axis runs over, the one named last changes fastest.
Arguments:
- queries: bfloat16 [1536, 768], P('query'), may hold values from -6 to 6
- label_ids: int32 [1536, 10], P('query'), may hold values from 0 to 4095, as said below
- label_text: bfloat16 [4096, 32, 768], P('label'), may hold values from -16 to 16
- up_weight: bfloat16 [768, 3072], P(None, 'query'), may hold values from -0.21875 to 0.21875
- down_weight: bfloat16 [768, 3072], P(None, 'query'), may hold values from -0.109375 to 0.109375
- free_vectors: float32 [4096, 768], P('label'), may hold values from -4 to 4
- moments: float32 [4096, 768], P('label'), may hold values from -0.06 to 0.06
- seconds: float32 [4096, 768], P('label'), may hold values from 1e-05 to 0.001
Outputs:
- free_new: float32 [4096, 768], P('label')
- moments_new: float32 [4096, 768], P('label')
- seconds_new: float32 [4096, 768], P('label')
- query_grad: float32 [1536, 768], P('query')
- up_grad: float32 [768, 3072], P('label', 'query')
- down_grad: float32 [768, 3072], P('label', 'query')
Inputs may be any that keep to these rules, and one draw needn't show every extreme that they name: `label_ids`: the 10 ids of one query are distinct.
All inputs are finite; a program needn't handle non-finite values.
Results may differ from a plain program's by a relative error of at most 0.023.
Values sent between devices are 32-bit elements; how exact they have to be, the bound alone decides.
A program may use at most 64 MiB of HBM per device.

v0:
```python
import jax
import jax.numpy as jnp
from jax import lax
from jax.sharding import PartitionSpec as P

beta_one = 0.9
beta_two = 0.999
adam_eps = 1e-08
learn_rate = 0.05
first_fix = 1.0 - 0.9**10
second_fix = 1.0 - 0.999**10


def gelu_tanh(values):
    return jax.nn.gelu(values, approximate=True)


def body(queries, label_ids, label_text, up_weight, down_weight, free_vectors, moments, seconds):
    label_rows, text_len, model_width = label_text.shape
    unit_cols = up_weight.shape[1]
    temper = 1.0 / jnp.sqrt(jnp.float32(model_width))
    text_rows = label_text.reshape(label_rows * text_len, model_width)
    preact = jnp.dot(text_rows, up_weight, preferred_element_type=jnp.float32)
    hidden = gelu_tanh(preact).astype(jnp.bfloat16)
    pooled_hidden = jnp.mean(
        hidden.reshape(label_rows, text_len, unit_cols), axis=1, dtype=jnp.float32
    )
    pooled_text = jnp.mean(label_text, axis=1, dtype=jnp.float32)
    encoded_part = jnp.einsum(
        "lf,df->ld", pooled_hidden, down_weight.astype(jnp.float32), precision=lax.Precision.HIGHEST
    )
    encoded = lax.psum(encoded_part, "query")
    label_vec = pooled_text + encoded + free_vectors
    label_bf = label_vec.astype(jnp.bfloat16)
    first_label = lax.axis_index("label") * label_rows
    local_ids = label_ids - first_label
    owners = (
        local_ids[:, :, None] == jnp.arange(label_rows, dtype=jnp.int32)[None, None, :]
    ).astype(jnp.float32)
    similar = jnp.einsum("id,jd->ij", queries, label_bf, preferred_element_type=jnp.float32)
    partial_value = jnp.einsum("ikj,ij->ik", owners, similar, precision=lax.Precision.HIGHEST)
    scores = lax.psum(partial_value, "label") * temper
    likely = jax.nn.softmax(scores, axis=-1)
    target = jnp.where(jnp.arange(scores.shape[1]) < 2, 0.5, 0.0).astype(jnp.float32)
    pair_coef = ((likely - target[None, :]) * temper).astype(jnp.bfloat16)
    spread = jnp.einsum(
        "ik,ikj->ij", pair_coef.astype(jnp.float32), owners, precision=lax.Precision.HIGHEST
    ).astype(jnp.bfloat16)
    query_terms = jnp.dot(spread, label_bf, preferred_element_type=jnp.float32)
    query_grad = lax.psum(query_terms, "label")
    grad_part = jnp.einsum("ij,id->jd", spread, queries, preferred_element_type=jnp.float32)
    count_part = jnp.sum(owners, axis=(0, 1))
    label_grad, counts = lax.psum((grad_part, count_part), "query")
    out_grad = label_grad.astype(jnp.bfloat16)
    hidden_grad = jnp.dot(out_grad, down_weight, preferred_element_type=jnp.float32) / text_len
    token_grad = jnp.broadcast_to(
        hidden_grad[:, None, :], (label_rows, text_len, unit_cols)
    ).reshape(label_rows * text_len, unit_cols)
    preact_grad = jax.vjp(gelu_tanh, preact)[1](token_grad)[0].astype(jnp.bfloat16)
    joined = lax.psum_scatter(
        jnp.concatenate(
            (
                lax.dot_general(
                    text_rows,
                    preact_grad,
                    (((0,), (0,)), ((), ())),
                    preferred_element_type=jnp.float32,
                ),
                jnp.einsum(
                    "ld,lf->df",
                    out_grad.astype(jnp.float32),
                    pooled_hidden,
                    precision=lax.Precision.HIGHEST,
                ),
            ),
            axis=1,
        ),
        "label",
        scatter_dimension=0,
        tiled=True,
    )
    up_part = joined[:, :unit_cols]
    down_part = joined[:, unit_cols:]
    touched = (counts > 0.5)[:, None]
    moment_step = beta_one * moments + (1.0 - beta_one) * label_grad
    second_step = beta_two * seconds + (1.0 - beta_two) * label_grad * label_grad
    update = (
        learn_rate * (moment_step / first_fix) / (jnp.sqrt(second_step / second_fix) + adam_eps)
    )
    free_new = jnp.where(touched, free_vectors - update, free_vectors)
    moments_new = jnp.where(touched, moment_step, moments)
    seconds_new = jnp.where(touched, second_step, seconds)
    return (free_new, moments_new, seconds_new, query_grad, up_part, down_part)


def solution(mesh):
    placed = (
        P("query", None),
        P("query", None),
        P("label", None, None),
        P(None, "query"),
        P(None, "query"),
        P("label", None),
        P("label", None),
        P("label", None),
    )
    return jax.shard_map(
        body,
        mesh=mesh,
        in_specs=placed,
        out_specs=(
            P("label", None),
            P("label", None),
            P("label", None),
            P("query", None),
            P("label", "query"),
            P("label", "query"),
        ),
        check_vma=False,
    )
```

profile of v0, /device:TPU:1, one launch (start us, length us, event | category | flops | bytes accessed | tf_op | source)
XLA Modules:
  0.0 642.2 jit_solution(12416014666471665310)
XLA Ops:
  7.2 0.0 copy-start
  7.2 0.0 all-reduce.6.cloned.1.call-start
  7.2 1.0 copy-done
  8.2 0.0 copy-start.2
  8.2 6.1 convert_reduce_fusion.1
  14.4 0.0 copy-start.8
  14.4 0.0 copy-start.5
  14.4 0.0 copy-start.4
  14.4 0.0 copy-done.2
  14.4 1.3 fusion.16
  15.7 0.0 all-reduce.6.cloned.1.call-update
  15.7 0.0 all-reduce.8.cloned.1.call-start
  15.8 2.9 convert_reduce_fusion
  18.7 0.0 copy-done.8
  18.7 76.4 %all-reduce.6.cloned.1.call-done = f32[64,768]{1,0:T(8,128)} async-done(((f32[64,768]{1,0:T(8,128)}), f32[64,768]{1,0:T(8,128)}) %all-reduce.6.cloned.1.call-update) | async-done | bytes 196624 | tf_op jit(solution)/shard_map/psum | solution.py:32
  95.1 0.0 copy-done.5
  95.1 1.0 add_convert_fusion
  96.1 0.0 copy-done.4
  96.1 0.2 convolution_bitcast_fusion.1
  96.3 0.1 select_reduce_fusion.1
  96.4 245.8 %psum.37 = f32[192,10]{0,1:T(8,128)S(1)} all-reduce(f32[192,10]{0,1:T(8,128)S(1)} %select_reduce_fusion.1), channel_id=1, replica_groups=mesh['label'=64,'query'=8] {'label'}, use_global_device_ids=true, to_apply=%region_5.0 | all-reduce | flops 1920 | bytes 15360 | tf_op jit(solution)/shard_map/psum | solution.py:42
  342.2 0.1 fusion.27
  342.3 0.2 convert_reduce_fusion.2
  342.5 0.1 copy.31
  342.7 0.9 fusion.32
  343.6 0.0 all-reduce.8.cloned.1.call-update
  343.6 0.0 all-reduce.10.cloned.1.call-start
  343.6 1.0 fusion.31
  344.7 73.6 %all-reduce.8.cloned.1.call-done = f32[64,768]{1,0:T(8,128)} async-done(((f32[64,768]{1,0:T(8,128)}), f32[64,768]{1,0:T(8,128)}) %all-reduce.8.cloned.1.call-update) | async-done | bytes 196624 | tf_op jit(solution)/shard_map/psum | solution.py:53
  418.2 0.0 copy-start.1
  418.2 1.3 convolution_multiply_fusion
  419.5 3.6 fusion.6
  423.1 0.0 copy-done.1
  423.1 0.0 copy-start.3
  423.1 1.4 convolution_bitcast_fusion
  424.6 0.0 copy-done.3
  424.6 0.7 fusion.14
  425.3 0.0 copy-start.6
  425.3 0.0 copy-start.7
  425.3 1.5 pad_maximum_fusion
  426.8 0.0 all-reduce.10.cloned.1.call-update
  426.9 1.3 dynamic-slice
  428.8 12.6 %psum.35 = f32[64]{0:T(128)S(1)} all-reduce(f32[64]{0:T(128)S(1)} %get-tuple-element.24), channel_id=1, replica_groups=mesh['label'=64,'query'=8] {'query'}, use_global_device_ids=true, to_apply=%region_1.0 | all-reduce | flops 64 | bytes 512 | tf_op jit(solution)/shard_map/psum | solution.py:53
  441.4 0.0 copy-done.6
  441.4 0.0 copy-done.7
  441.4 1.0 fusion.13
  442.4 188.6 %all-reduce.10.cloned.1.call-done = (f32[192,768]{1,0:T(8,128)}, f32[768,768]{0,1:T(8,128)}) async-done(((f32[192,768]{1,0:T(8,128)}, f32[768,768]{0,1:T(8,128)}), (f32[192,768]{1,0:T(8,128)}, f32[768,768]{0,1:T(8,128)})) %all-reduce.10.cloned.1.call-update) | async-done | bytes 2949136 | tf_op jit(solution)/shard_map/psum | solution.py:50
  631.0 1.3 fusion.30
  632.3 0.7 copy.20
  633.0 0.7 copy.21
  633.7 1.9 copy.41
  (5 shorter events, 0.1 us)
Async XLA Ops:
  7.2 1.1 copy-start
  7.2 87.9 %all-reduce.6.cloned.1.call-start = ((), (), s32[]{:S(2)}) async-start(), calls=%async_computation | async-start | bytes 393216 | tf_op jit(solution)/shard_map/psum | solution.py:32
  8.2 6.1 copy-start.2
  14.4 4.3 copy-start.8
  14.4 80.8 %copy-start.5 = (f32[64,768]{1,0:T(8,128)S(1)}, f32[64,768]{1,0:T(8,128)}, u32[]{:S(2)}) copy-start(f32[64,768]{1,0:T(8,128)} %param.13) | copy-start | bytes 589828
  14.4 81.7 %copy-start.4 = (bf16[192,768]{1,0:T(8,128)(2,1)S(1)}, bf16[192,768]{1,0:T(8,128)(2,1)}, u32[]{:S(2)}) copy-start(bf16[192,768]{1,0:T(8,128)(2,1)} %param.8) | copy-start | bytes 884740
  15.7 402.5 %all-reduce.8.cloned.1.call-start = ((), (), s32[]{:S(2)}) async-start(), calls=%async_computation.1 | async-start | bytes 393216 | tf_op jit(solution)/shard_map/psum | solution.py:53
  343.6 287.4 %all-reduce.10.cloned.1.call-start = ((), (), s32[]{:S(2)}) async-start(), calls=%async_computation.2 | async-start | bytes 5898240 | tf_op jit(solution)/shard_map/psum | solution.py:50
  418.2 4.9 copy-start.1
  423.1 1.5 copy-start.3
  425.3 16.2 %copy-start.6 = (f32[64,768]{1,0:T(8,128)S(1)}, f32[64,768]{1,0:T(8,128)}, u32[]{:S(2)}) copy-start(f32[64,768]{1,0:T(8,128)} %param.15) | copy-start | bytes 589828
  425.3 16.2 %copy-start.7 = (f32[64,768]{1,0:T(8,128)S(1)}, f32[64,768]{1,0:T(8,128)}, u32[]{:S(2)}) copy-start(f32[64,768]{1,0:T(8,128)} %param.14) | copy-start | bytes 589828
Sparse Core Ops, SparseCore 0:
  15.8 79.2 all-reduce.5
  343.7 74.4 all-reduce.7
  427.0 203.9 all-reduce.9
where the time goes:
time: 644 us; the launch traced here: 642 us
  waiting for transfers between devices  339 us (53%)
  blocking collectives  258 us (40%)
  between operations  14.6 us (2%)
  matrix products  13 us (2%)
  other arithmetic  10.4 us (2%)
  local copies, waits for them, and re-layouts  7.07 us (1%)
    psum x1, blocking collectives, body(): scores = lax.psum(partial_value, 'label') * temper  246 us
    psum x1, waiting for transfers between devices, body(): query_grad = lax.psum(query_terms, 'label')  189 us
    psum x1, waiting for transfers between devices, body(): encoded = lax.psum(encoded_part, 'query')  76.4 us
    psum x1, waiting for transfers between devices, body(): label_grad, counts = lax.psum((grad_part, count_part), 'query')  73.6 us
  transfers between devices with their start and end apart: 3, of which 3 were waited for; matrix products, arithmetic and copies ran while one was open for 1% of the time, Pallas kernels for 0%

commit v1 on v0

v1 whole, which is shorter than its diff:
```python
import functools
import math

import jax
import jax.numpy as jnp
from jax import lax
from jax.experimental import pallas as pl
from jax.experimental.pallas import tpu as pltpu
from jax.sharding import PartitionSpec as P

MESH = pl.DeviceIdType.MESH
F32 = jnp.float32
BF16 = jnp.bfloat16

beta_one = 0.9
beta_two = 0.999
adam_eps = 1e-08
learn_rate = 0.05
first_fix = 1.0 - 0.9**10
second_fix = 1.0 - 0.999**10
ROOT = math.sqrt(2.0 / math.pi)
CUBIC = 0.044715

NT = (((1,), (1,)), ((), ()))
TN = (((0,), (0,)), ((), ()))


def far_first(count):
    return sorted(range(1, count), key=lambda o: (-min(o, count - o), o))


def kernel(
    dims,
    queries_h,
    ids_h,
    text_h,
    up_h,
    down_h,
    free_h,
    mom_h,
    sec_h,
    free_o,
    mom_o,
    sec_o,
    query_o,
    up_o,
    down_o,
    text,
    text_t,
    upw,
    dnw,
    qp,
    ids,
    fre,
    mom,
    sec,
    slope,
    pooled,
    enc,
    enc_in,
    lvec,
    lbf,
    idp,
    idt,
    idpack,
    cnt,
    cnt_in,
    sc_c,
    sc_x,
    sc_y,
    sc_c_in,
    sc_x_in,
    sc_y_in,
    lg_part,
    lg_in,
    lg,
    qt,
    q_c_in,
    q_one,
    q_x_in,
    q_two,
    q_y_in,
    q_four,
    q_five,
    q_six,
    pgrad,
    wpart,
    w_c_in,
    w_one,
    w_x_in,
    w_two,
    w_y_in,
    w_give,
    w_got,
    w_out,
    free_n,
    mom_n,
    sec_n,
    in_sem,
    text_sem,
    out_sem,
    enc_ss,
    enc_rs,
    lv_ss,
    lv_rs,
    cnt_ss,
    cnt_rs,
    sc_ss,
    sc_rs,
    lgr_ss,
    lgr_rs,
    lga_ss,
    lga_rs,
    q_ss,
    q_rs,
    w_ss,
    w_rs,
):
    ny, nx, nc, nz = dims
    lab = lax.axis_index("label")
    z = lax.axis_index("query")
    y = lab // (nx * nc)
    x = (lab // nc) % nx
    c = lab % nc
    other = 1 - c
    offs_z, offs_y, offs_x = far_first(nz), far_first(ny), far_first(nx)
    labels, width = lvec.shape
    units = upw.shape[1]
    tokens = text.shape[0] // labels
    lz = labels // nz
    rows_z = text.shape[0] // nz

    def at_z(o):
        return (lab, (z + o) % nz)

    def at_y(o):
        return (((y + o) % ny * nx + x) * nc + c, z)

    def at_x(o):
        return ((y * nx + (x + o) % nx) * nc + c, z)

    at_core = ((y * nx + x) * nc + other, z)

    barrier = pltpu.get_barrier_semaphore()
    peers = (
        [at_z(o) for o in offs_z]
        + [at_y(o) for o in offs_y]
        + [at_x(o) for o in offs_x]
        + [at_core]
    )
    for peer in peers:
        pl.semaphore_signal(barrier, inc=1, device_id=peer, device_id_type=MESH)

    def remote(src, dst, ss, rs, peer):
        return pltpu.make_async_remote_copy(
            src_ref=src,
            dst_ref=dst,
            send_sem=ss,
            recv_sem=rs,
            device_id=peer,
            device_id_type=MESH,
        )

    def offset_of(t):
        return (nz // 2 + (1 - 2 * (t % 2)) * ((t + 1) // 2)) % nz

    def text_copy(t):
        j = (z + offset_of(t)) % nz
        rows = pl.ds(pl.multiple_of(j * rows_z, rows_z), rows_z)
        return pltpu.make_async_copy(text_h.at[rows], text.at[rows], text_sem.at[t])

    in_copies = [
        pltpu.make_async_copy(src, dst, in_sem.at[i])
        for i, (src, dst) in enumerate(
            (
                (up_h, upw),
                (down_h, dnw),
                (free_h, fre),
                (ids_h, ids),
                (queries_h, qp.at[pl.ds(0, 192)]),
                (queries_h.at[pl.ds(128, 64)], qp.at[pl.ds(192, 64)]),
                (mom_h, mom),
                (sec_h, sec),
            )
        )
    ]
    in_copies[0].start()
    text_copy(0).start()
    in_copies[1].start()

    def start_text(t, carry):
        text_copy(t).start()
        return carry

    lax.fori_loop(1, nz, start_text, 0)
    for copy in in_copies[2:]:
        copy.start()
    in_copies[0].wait()

    def encode(t):
        o = offset_of(t)
        j = (z + o) % nz
        text_copy(t).wait()
        hidden = []
        for half in range(2):
            rows = pl.ds(pl.multiple_of(j * rows_z + half * (rows_z // 2), rows_z // 2), rows_z // 2)
            pre = jnp.dot(text[rows, :], upw[...], preferred_element_type=F32)
            square = pre * pre
            bent = jnp.tanh(pre * (ROOT + (ROOT * CUBIC) * square))
            gate = 0.5 + 0.5 * bent
            hidden.append(pre * gate)
            slope[rows, :] = gate + (0.5 * pre) * (1.0 - bent * bent) * (
                ROOT + (3.0 * ROOT * CUBIC) * square
            )
        hidden = jnp.concatenate(hidden, axis=0)
        mean = jnp.sum(hidden.reshape(lz, tokens, units), axis=1) * (1.0 / tokens)
        pooled[pl.ds(pl.multiple_of(j * lz, lz), lz), :] = mean
        rest = mean - mean.astype(BF16).astype(F32)
        both = jnp.concatenate([mean, rest], axis=0).astype(BF16)
        out = lax.dot_general(both, dnw[...], NT, preferred_element_type=F32)
        enc[o] = out[:lz] + out[lz:]

    def enc_copy(t):
        o = offset_of(t)
        return remote(enc.at[o], enc_in.at[o], enc_ss.at[o], enc_rs.at[o], at_z(o))

    def encode_step(t, carry):
        encode(t)
        return carry

    def send_step(t, carry):
        enc_copy(t).start()
        return carry

    def encode_send_step(t, carry):
        encode(t)
        enc_copy(t).start()
        return carry

    early = min(2, nz - 1)
    in_copies[1].wait()
    lax.fori_loop(0, early, encode_step, 0)
    pl.semaphore_wait(barrier, len(peers))
    lax.fori_loop(0, early, send_step, 0)
    lax.fori_loop(early, nz - 1, encode_send_step, 0)
    encode(nz - 1)
    own_text = pl.ds(pl.multiple_of(z * rows_z, rows_z), rows_z)
    own_rows = pl.ds(pl.multiple_of(z * lz, lz), lz)
    text_mean = jnp.sum(text[own_text, :].astype(F32).reshape(lz, tokens, width), axis=1) * (1.0 / tokens)
    in_copies[2].wait()
    total = enc[0] + text_mean + fre[own_rows, :]
    for o in offs_z:
        remote(enc.at[o], enc_in.at[o], enc_ss.at[o], enc_rs.at[o], at_z(o)).wait_recv()
        total += enc_in[o]
    lvec[own_rows, :] = total
    lv_copies = [
        remote(lvec.at[own_rows], lvec.at[own_rows], lv_ss.at[o], lv_rs.at[o], at_z(o)) for o in offs_z
    ]
    for copy in lv_copies:
        copy.start()

    in_copies[3].wait()
    idp[...] = jnp.full(idp.shape, -1.0, F32)
    local = (ids[...] - lab * labels).astype(F32)
    idp[0:192, 0:10] = local
    idp[192:256, 0:10] = local[128:192]
    idt[...] = jnp.transpose(idp[...])
    lane = lax.broadcasted_iota(jnp.int32, (1, 128), 1)
    idpack[...] = jnp.full(idpack.shape, -1.0, F32)
    idpack[0:10, :] = idt[0:10, 0:128]
    for r in range(5):
        idpack[10 + r : 11 + r, :] = jnp.where(lane < 64, idt[r : r + 1, 128:256], idt[r + 5 : r + 6, 128:256])

    def owned(p, count):
        slots = lax.broadcasted_iota(jnp.int32, (count, 128), 0).astype(F32)
        return idpack[p : p + 1, :] == slots

    def packed(rows):
        acc = jnp.zeros((128, 128), F32)
        for p in rows:
            acc += jnp.where(owned(p, 128), 1.0, 0.0)
        return acc.astype(BF16)

    ones = jnp.ones((8, 128), BF16)
    cnt[...] = lax.dot_general(ones, packed(range(10)), NT, preferred_element_type=F32) + lax.dot_general(
        ones, packed(range(10, 15)), NT, preferred_element_type=F32
    )
    cnt_copies = [remote(cnt, cnt_in.at[o], cnt_ss.at[o], cnt_rs.at[o], at_z(o)) for o in offs_z]
    for copy in cnt_copies:
        copy.start()

    def turn(t, carry):
        rows = pl.ds(pl.multiple_of(t * 256, 256), 256)
        text_t[:, rows] = jnp.transpose(text[rows, :])
        return carry

    lax.fori_loop(0, text.shape[0] // 256, turn, 0)
    in_copies[4].wait()
    in_copies[5].wait()

    for copy in lv_copies:
        copy.wait_recv()
    lbf[...] = lvec[...].astype(BF16)

    similar = lax.dot_general(lbf[...], qp[...], NT, preferred_element_type=F32)
    sc_c[...] = jnp.zeros(sc_c.shape, F32)
    for p in range(15):
        block = similar[:, 0:128] if p < 10 else similar[:, 128:256]
        sc_c[p : p + 1, :] = jnp.sum(jnp.where(owned(p, labels), block, 0.0), axis=0, keepdims=True)
    score_copies = []

    def exchange(src, dst, base, offs, at):
        copies = [
            remote(src, dst.at[o], sc_ss.at[base + o], sc_rs.at[base + o], at(o)) for o in offs
        ]
        score_copies.extend(copies)
        for copy in copies:
            copy.start()
        acc = src[...]
        for copy, o in zip(copies, offs):
            copy.wait_recv()
            acc += dst[o]
        return acc

    sc_x[...] = exchange(sc_c, sc_c_in, 0, [1], lambda o: at_core)
    sc_y[...] = exchange(sc_x, sc_x_in, 2, offs_x, at_x)
    scores = exchange(sc_y, sc_y_in, 2 + nx, offs_y, at_y)

    temper = 1.0 / math.sqrt(width)
    scores = scores * temper
    top, low = scores[0:10], scores[10:15]
    top_max = jnp.max(top, axis=0, keepdims=True)
    low_max = jnp.max(low, axis=0, keepdims=True)
    low_max = jnp.maximum(low_max, pltpu.roll(low_max, 64, 1))
    top = jnp.exp(top - top_max)
    low = jnp.exp(low - low_max)
    top_sum = jnp.sum(top, axis=0, keepdims=True)
    low_sum = jnp.sum(low, axis=0, keepdims=True)
    low_sum = low_sum + pltpu.roll(low_sum, 64, 1)
    row_t = lax.broadcasted_iota(jnp.int32, (10, 128), 0)
    row_l = lax.broadcasted_iota(jnp.int32, (5, 128), 0)
    lane_l = lax.broadcasted_iota(jnp.int32, (5, 128), 1)
    top = (top / top_sum - jnp.where(row_t < 2, 0.5, 0.0)) * temper
    low = (low / low_sum - jnp.where((row_l < 2) & (lane_l < 64), 0.5, 0.0)) * temper
    top = top.astype(BF16).astype(F32)
    low = low.astype(BF16).astype(F32)
    spread = []
    for coef, base in ((top, 0), (low, 10)):
        acc = jnp.zeros((labels, 128), F32)
        for k in range(coef.shape[0]):
            acc += jnp.where(owned(base + k, labels), coef[k : k + 1], 0.0)
        spread.append(acc)
    spread = jnp.concatenate(spread, axis=1).astype(BF16)

    lg_part[...] = jnp.dot(spread, qp[...], preferred_element_type=F32)
    lgr_copies = []
    for o in offs_z:
        rows = pl.ds(pl.multiple_of((z + o) % nz * lz, lz), lz)
        lgr_copies.append(remote(lg_part.at[rows], lg_in.at[o], lgr_ss.at[o], lgr_rs.at[o], at_z(o)))
        lgr_copies[-1].start()

    terms = lax.dot_general(spread, lbf[...], TN, preferred_element_type=F32)
    for half in range(2):
        cols = slice(half * (width // 2), (half + 1) * (width // 2))
        qt[half, 0:128, :] = terms[0:128, cols]
        qt[half, 128:192, :] = terms[128:192, cols] + terms[192:256, cols]
    q_core = remote(qt.at[other], q_c_in, q_ss.at[0], q_rs.at[0], at_core)
    q_core.start()
    qx = 192 // nx
    owners = 6 if ny == 8 else ny
    qy = qx // owners
    q_core.wait_recv()
    q_one[...] = qt[c] + q_c_in[...]
    q_x_copies = []
    for o in offs_x:
        rows = pl.ds(pl.multiple_of((x + o) % nx * qx, qx), qx)
        q_x_copies.append(remote(q_one.at[rows], q_x_in.at[o], q_ss.at[1 + o], q_rs.at[1 + o], at_x(o)))
        q_x_copies[-1].start()

    total = lg_part[own_rows, :]
    for copy, o in zip(lgr_copies, offs_z):
        copy.wait_recv()
        total += lg_in[o]
    lg[own_rows, :] = total
    lga_copies = [remote(lg.at[own_rows], lg.at[own_rows], lga_ss.at[o], lga_rs.at[o], at_z(o)) for o in offs_z]
    for copy in lga_copies:
        copy.start()

    acc = q_one[pl.ds(pl.multiple_of(x * qx, qx), qx), :]
    for copy, o in zip(q_x_copies, offs_x):
        copy.wait_recv()
        acc += q_x_in[o]
    q_two[...] = acc
    base_y = 1 + nx
    base_g = base_y + ny

    def q_y_copy(b):
        o = (b - y + ny) % ny
        return o, remote(
            q_two.at[pl.ds(b * qy, qy)],
            q_y_in.at[o],
            q_ss.at[base_y + b],
            q_rs.at[base_y + o],
            ((b * nx + x) * nc + c, z),
        )

    for b in range(owners):
        o, copy = q_y_copy(b)

        @pl.when(o != 0)
        def _():
            copy.start()

    seen = cnt[...]
    for copy, o in zip(cnt_copies, offs_z):
        copy.wait_recv()
        seen += cnt_in[o]
    diag = lax.broadcasted_iota(jnp.int32, (labels, 128), 0) == lax.broadcasted_iota(
        jnp.int32, (labels, 128), 1
    )
    touched = jnp.sum(jnp.where(diag, seen[0:1], 0.0), axis=1, keepdims=True) > 0.5

    for copy in lga_copies:
        copy.wait_recv()
    grad = lg[...]
    out_grad = grad.astype(BF16)
    hidden_grad = jnp.dot(out_grad, dnw[...], preferred_element_type=F32) * (1.0 / tokens)

    mean = pooled[...]
    rest = mean - mean.astype(BF16).astype(F32)
    both = jnp.concatenate([mean, rest], axis=0).astype(BF16)
    twice = jnp.concatenate([out_grad, out_grad], axis=0)
    down_part = lax.dot_general(twice, both, TN, preferred_element_type=F32)
    wpart[0] = down_part.reshape(wpart.shape[1:])
    w_core = [remote(wpart.at[k, other], w_c_in.at[k], w_ss.at[k, 0], w_rs.at[k, 0], at_core) for k in range(2)]
    w_core[0].start()

    for j in range(nz):
        rows = slice(j * rows_z, (j + 1) * rows_z)
        spreaded = jnp.broadcast_to(
            hidden_grad[j * lz : (j + 1) * lz, None, :], (lz, tokens, units)
        ).reshape(rows_z, units)
        pgrad[rows, :] = (slope[rows, :] * spreaded).astype(BF16)

    half_rows = width // nc

    def up_half(h):
        rows = pl.ds(pl.multiple_of(h * half_rows, half_rows), half_rows)
        part = jnp.dot(text_t[rows, :], pgrad[...], preferred_element_type=F32)
        wpart[1, h] = part.reshape(wpart.shape[2:])

    up_half(other)
    w_core[1].start()

    w_x_copies = [[], []]

    def across_x(k):
        w_core[k].wait_recv()
        w_one[k] = wpart[k, c] + w_c_in[k]
        for o in offs_x:
            copy = remote(
                w_one.at[k, :, (x + o) % nx],
                w_x_in.at[k, o],
                w_ss.at[k, 1 + o],
                w_rs.at[k, 1 + o],
                at_x(o),
            )
            copy.start()
            w_x_copies[k].append(copy)

    across_x(0)
    up_half(c)
    across_x(1)

    @pl.when(y < owners)
    def _():
        acc = q_two[pl.ds(pl.multiple_of(y % owners * qy, qy), qy), :]
        for o in offs_y:
            remote(
                q_two.at[pl.ds(0, qy)], q_y_in.at[o], q_ss.at[base_y], q_rs.at[base_y + o], at_y(o)
            ).wait_recv()
            acc += q_y_in[o]
        mine = pl.ds(pl.multiple_of(y % owners * qy, qy), qy)
        q_four[mine, :] = acc
        for o in offs_y:
            remote(
                q_four.at[mine], q_four.at[mine], q_ss.at[base_g + o], q_rs.at[base_g + y], at_y(o)
            ).start()

    in_copies[6].wait()
    in_copies[7].wait()
    moment = beta_one * mom[...] + (1.0 - beta_one) * grad
    second = beta_two * sec[...] + (1.0 - beta_two) * grad * grad
    update = learn_rate * (moment / first_fix) / (jnp.sqrt(second / second_fix) + adam_eps)
    free_n[...] = jnp.where(touched, fre[...] - update, fre[...])
    mom_n[...] = jnp.where(touched, moment, mom[...])
    sec_n[...] = jnp.where(touched, second, sec[...])
    out_copies = [
        pltpu.make_async_copy(src, dst, out_sem.at[i])
        for i, (src, dst) in enumerate(((free_n, free_o), (mom_n, mom_o), (sec_n, sec_o)))
    ]
    for copy in out_copies:
        copy.start()

    for b in range(owners):

        @pl.when(y != b)
        def _():
            rows = pl.ds(b * qy, qy)
            remote(
                q_four.at[rows], q_four.at[rows], q_ss.at[base_g], q_rs.at[base_g + b], at_core
            ).wait_recv()

    own_x = pl.ds(pl.multiple_of(x * qx, qx), qx)
    q_five[own_x, :] = q_four[...]
    base_h = base_g + ny
    q_xg_copies = [
        remote(q_four, q_five.at[own_x], q_ss.at[base_h + o], q_rs.at[base_h + o], at_x(o)) for o in offs_x
    ]
    for copy in q_xg_copies:
        copy.start()

    per_core = ny // nc

    def w_y_copy(k, b):
        goal = c * per_core + b
        o = (goal - y + ny) % ny
        return o, remote(
            w_two.at[k, b],
            w_y_in.at[k, o],
            w_ss.at[k, 1 + nx + b],
            w_rs.at[k, 1 + nx + o],
            ((goal * nx + x) * nc + c, z),
        )

    def across_y(k):
        acc = w_one[k, :, x]
        for copy, o in zip(w_x_copies[k], offs_x):
            copy.wait_recv()
            acc += w_x_in[k, o]
        w_two[k] = acc
        for b in range(per_core):
            o, copy = w_y_copy(k, b)

            @pl.when(o != 0)
            def _():
                copy.start()

    across_y(0)
    across_y(1)

    for copy in q_xg_copies:
        copy.wait_recv()
    q_back = remote(q_five, q_six, q_ss.at[base_h + nx], q_rs.at[base_h + nx], at_core)
    q_back.start()

    holder = y // per_core == c
    rows_out = w_out.shape[1]

    def w_last(k):
        return remote(
            w_give.at[k], w_got.at[k], w_ss.at[k, 1 + nx + ny], w_rs.at[k, 1 + nx + ny], at_core
        )

    for k in range(2):

        @pl.when(holder)
        def _():
            acc = w_two[k, y % per_core]
            for o in offs_y:
                remote(
                    w_two.at[k, 0], w_y_in.at[k, o], w_ss.at[k, 0], w_rs.at[k, 1 + nx + o], at_y(o)
                ).wait_recv()
                acc += w_y_in[k, o]
            first, last = acc[:rows_out], acc[rows_out:]
            w_give[k, 0:rows_out, :] = jnp.where(c == 0, last, first)
            w_last(k).start()
            w_out[k] = jnp.where(c == 0, first, last)

    for half in range(2):
        cols = slice(half * (width // 2), (half + 1) * (width // 2))

        @pl.when(c == half)
        def _():
            pltpu.make_async_copy(q_five, query_o.at[:, cols], out_sem.at[3]).start()

    q_back.wait_recv()
    for half in range(2):
        cols = slice(half * (width // 2), (half + 1) * (width // 2))

        @pl.when(other == half)
        def _():
            pltpu.make_async_copy(q_six, query_o.at[:, cols], out_sem.at[4]).start()

    for k in range(2):

        @pl.when(jnp.logical_not(holder))
        def _():
            w_last(k).wait_recv()
            w_out[k] = w_got[k, 0:rows_out, :]

    w_writes = [
        pltpu.make_async_copy(w_out.at[0], down_o, out_sem.at[5]),
        pltpu.make_async_copy(w_out.at[1], up_o, out_sem.at[6]),
    ]
    for copy in w_writes:
        copy.start()

    for o in offs_z:
        remote(enc.at[o], enc_in.at[o], enc_ss.at[o], enc_rs.at[o], at_z(o)).wait_send()
    for copy in (
        lv_copies + cnt_copies + score_copies + lgr_copies + lga_copies + q_x_copies + q_xg_copies
        + w_core + w_x_copies[0] + w_x_copies[1] + [q_core, q_back]
    ):
        copy.wait_send()
    for b in range(owners):
        o, copy = q_y_copy(b)

        @pl.when(o != 0)
        def _():
            copy.wait_send()

    @pl.when(y < owners)
    def _():
        mine = pl.ds(pl.multiple_of(y % owners * qy, qy), qy)
        for o in offs_y:
            remote(
                q_four.at[mine], q_four.at[mine], q_ss.at[base_g + o], q_rs.at[base_g + y], at_y(o)
            ).wait_send()

    for k in range(2):
        for b in range(per_core):
            o, copy = w_y_copy(k, b)

            @pl.when(o != 0)
            def _():
                copy.wait_send()

        @pl.when(holder)
        def _():
            w_last(k).wait_send()

    for copy in out_copies + w_writes:
        copy.wait()
    pltpu.make_async_copy(q_five, query_o.at[:, 0 : width // 2], out_sem.at[3]).wait()
    pltpu.make_async_copy(q_six, query_o.at[:, 0 : width // 2], out_sem.at[4]).wait()


def body(dims, queries, label_ids, label_text, up_weight, down_weight, free_vectors, moments, seconds):
    ny, nx, nc, nz = dims
    labels, tokens, width = label_text.shape
    units = up_weight.shape[1]
    rows = labels * tokens
    text_rows = label_text.reshape(rows, width)
    lz = labels // nz
    rows_out = width // (ny * nx * nc)
    chip_rows = rows_out * nc
    per_core = ny // nc
    half = width // 2
    qx = 192 // nx
    qy = qx // (6 if ny == 8 else ny)
    staged = -(-rows_out // 8) * 8
    vmem = pltpu.VMEM
    dma = pltpu.SemaphoreType.DMA
    scratch = [
        vmem((rows, width), BF16),
        vmem((width, rows), BF16),
        vmem((width, units), BF16),
        vmem((width, units), BF16),
        vmem((256, width), BF16),
        vmem((192, 10), jnp.int32),
        vmem((labels, width), F32),
        vmem((labels, width), F32),
        vmem((labels, width), F32),
        vmem((rows, units), F32),
        vmem((labels, units), F32),
        vmem((nz, lz, width), F32),
        vmem((nz, lz, width), F32),
        vmem((labels, width), F32),
        vmem((labels, width), BF16),
        vmem((256, 128), F32),
        vmem((128, 256), F32),
        vmem((16, 128), F32),
        vmem((8, 128), F32),
        vmem((nz, 8, 128), F32),
        vmem((16, 128), F32),
        vmem((16, 128), F32),
        vmem((16, 128), F32),
        vmem((2, 16, 128), F32),
        vmem((nx, 16, 128), F32),
        vmem((ny, 16, 128), F32),
        vmem((labels, width), F32),
        vmem((nz, lz, width), F32),
        vmem((labels, width), F32),
        vmem((2, 192, half), F32),
        vmem((192, half), F32),
        vmem((192, half), F32),
        vmem((nx, qx, half), F32),
        vmem((qx, half), F32),
        vmem((ny, qy, half), F32),
        vmem((qx, half), F32),
        vmem((192, half), F32),
        vmem((192, half), F32),
        vmem((rows, units), BF16),
        vmem((2, nc, per_core, nx, chip_rows, units), F32),
        vmem((2, per_core, nx, chip_rows, units), F32),
        vmem((2, per_core, nx, chip_rows, units), F32),
        vmem((2, nx, per_core, chip_rows, units), F32),
        vmem((2, per_core, chip_rows, units), F32),
        vmem((2, ny, chip_rows, units), F32),
        vmem((2, staged, units), F32),
        vmem((2, staged, units), F32),
        vmem((2, rows_out, units), F32),
        vmem((labels, width), F32),
        vmem((labels, width), F32),
        vmem((labels, width), F32),
        dma((8,)),
        dma((nz,)),
        dma((7,)),
        dma((nz,)),
        dma((nz,)),
        dma((nz,)),
        dma((nz,)),
        dma((nz,)),
        dma((nz,)),
        dma((2 + nx + ny,)),
        dma((2 + nx + ny,)),
        dma((nz,)),
        dma((nz,)),
        dma((nz,)),
        dma((nz,)),
        dma((2 + 2 * nx + 2 * ny,)),
        dma((2 + 2 * nx + 2 * ny,)),
        dma((2, 2 + nx + ny)),
        dma((2, 2 + nx + ny)),
    ]
    hbm = pl.BlockSpec(memory_space=pl.ANY)
    flops = 2 * rows * width * units * 2
    return pl.pallas_call(
        functools.partial(kernel, dims),
        out_shape=[
            jax.ShapeDtypeStruct((labels, width), F32),
            jax.ShapeDtypeStruct((labels, width), F32),
            jax.ShapeDtypeStruct((labels, width), F32),
            jax.ShapeDtypeStruct((192, width), F32),
            jax.ShapeDtypeStruct((rows_out, units), F32),
            jax.ShapeDtypeStruct((rows_out, units), F32),
        ],
        in_specs=[hbm] * 8,
        out_specs=[hbm] * 6,
        scratch_shapes=scratch,
        name="step",
        cost_estimate=pl.CostEstimate(flops=flops, bytes_accessed=8 * 2**20, transcendentals=rows * units),
        compiler_params=pltpu.CompilerParams(
            collective_id=0, has_side_effects=True, vmem_limit_bytes=56 * 2**20
        ),
    )(queries, label_ids, text_rows, up_weight, down_weight, free_vectors, moments, seconds)


def build(mesh, dims):
    placed = (
        P("query", None),
        P("query", None),
        P("label", None, None),
        P(None, "query"),
        P(None, "query"),
        P("label", None),
        P("label", None),
        P("label", None),
    )
    return jax.shard_map(
        functools.partial(body, dims),
        mesh=mesh,
        in_specs=placed,
        out_specs=(
            P("label", None),
            P("label", None),
            P("label", None),
            P("query", None),
            P("label", "query"),
            P("label", "query"),
        ),
        check_vma=False,
    )


def solution(mesh):
    return build(mesh, (8, 4, 2, mesh.shape["query"]))
```

time: 644 us -> 88.6 us (0.14)
  waiting for transfers between devices: 339 us -> 0 us
  blocking collectives: 258 us -> 0 us
  Pallas kernels: 0 us -> 76.7 us
  between operations: 14.6 us -> 0.64 us
  matrix products: 13 us -> 0 us
  other arithmetic: 10.4 us -> 0 us
    psum x3 -> x0, waiting for transfers between devices: 339 us -> none  [the longest x1 189 us: body(): query_grad = lax.psum(query_terms, 'label')]
    psum x2 -> x0, blocking collectives: 258 us -> none  [the longest x1 246 us: body(): scores = lax.psum(partial_value, 'label') * temper]
    pallas_call x0 -> x1, Pallas kernels: none -> 76.7 us  [body(): pl.pallas_call(functools.partial(kernel, dims), out_shape=[jax.ShapeDtype...]
    dot_general x8 -> x0, matrix products: 13 us -> none  [the longest x1 6.12 us: body(): preact = jnp.dot(text_rows, up_weight, preferred_element_type=jnp.float32)]
  transfers between devices with their start and end apart: 3 -> 0, of which waited for: 3 -> 0; matrix products, arithmetic and copies ran while one was open for 1% -> 0% of each run, Pallas kernels for 0% -> 0%
where the time goes in v1:
time: 88.6 us; the launch traced here: 88.2 us
  Pallas kernels  76.7 us (87%)
  local copies, waits for them, and re-layouts  10.9 us (12%)
    pallas_call x1, Pallas kernels, body(): pl.pallas_call(functools.partial(kernel, dims), out_shape=[jax.ShapeDtype...  76.7 us
    unnamed x7, local copies, waits for them, and re-layouts  10.9 us

profile of v1, /device:TPU:1, one launch (start us, length us, event | category | flops | bytes accessed | tf_op | source)
XLA Modules:
  0.0 88.2 jit_solution(6787457194112044010)
XLA Ops:
  0.6 1.5 %copy.14.ids_h = s32[192,10]{1,0:T(8,128)} copy(s32[192,10]{0,1:T(8,128)} %param.9) | data formatting | bytes 15360 | tf_op args[1]
  2.1 76.7 %step.1 = (f32[64,768]{1,0:T(8,128)}, f32[64,768]{1,0:T(8,128)}, f32[64,768]{1,0:T(8,128)}, f32[192,768]{1,0:T(8,128)}, f32[12,384]{1,0:T(8,128)}, /*index=5*/f32[12,384]{1,0:T(8,128)}) custom-call(bf16[192,768]{1,0:T(8,128)(2,1)} %queries_h.1, s32[192,10]{1,0:T(8,128)} %copy.14.ids_h, bf16[2048,768]{1,0:T(8,128)(2,1)} %bitcast.1, bf16[768,384]{1,0:T(8,128)(2,1)} %up_h.1, ...), custom_call_target="tpu_custom_call" | custom-call | flops 2415919104 | bytes 8388608 | tf_op jit(solution)/shard_map/step/pallas_call | solution.py:739
  78.8 1.6 %copy.21 = f32[64,768]{1,0:T(8,128)} copy(f32[64,768]{1,0:T(8,128)} %get-tuple-element.12) | data formatting | bytes 393216
  80.4 1.6 %copy.22 = f32[64,768]{1,0:T(8,128)} copy(f32[64,768]{1,0:T(8,128)} %get-tuple-element.13) | data formatting | bytes 393216
  82.0 1.6 %copy.23 = f32[64,768]{1,0:T(8,128)} copy(f32[64,768]{1,0:T(8,128)} %get-tuple-element.14) | data formatting | bytes 393216
  83.6 1.9 %copy.24 = f32[192,768]{1,0:T(8,128)} copy(f32[192,768]{1,0:T(8,128)} %get-tuple-element.15) | data formatting | bytes 1179648
  85.5 1.3 %copy.25 = f32[12,384]{1,0:T(8,128)} copy(f32[12,384]{1,0:T(8,128)} %get-tuple-element.16) | data formatting | bytes 36864
  86.9 1.3 %copy.26 = f32[12,384]{1,0:T(8,128)} copy(f32[12,384]{1,0:T(8,128)} %get-tuple-element.17) | data formatting | bytes 36864

commit v2 on v1

--- a/solution.py
+++ b/solution.py
@@ -55,7 +55,8 @@
     mom,
     sec,
     slope,
-    pooled,
+    pool_in,
+    pool_bf,
     enc,
     enc_in,
     lvec,
@@ -77,21 +78,20 @@
     qt,
     q_c_in,
     q_one,
+    q_y_in,
     q_x_in,
-    q_two,
-    q_y_in,
-    q_four,
     q_five,
     q_six,
+    lg_pair,
+    og_t,
+    og_in,
     pgrad,
-    wpart,
-    w_c_in,
-    w_one,
-    w_x_in,
+    upart,
+    u_c_in,
+    u_one,
+    u_x_in,
     w_two,
     w_y_in,
-    w_give,
-    w_got,
     w_out,
     free_n,
     mom_n,
@@ -113,6 +113,12 @@
     lga_rs,
     q_ss,
     q_rs,
+    pool_ss,
+    pool_rs,
+    og_ss,
+    og_rs,
+    u_ss,
+    u_rs,
     w_ss,
     w_rs,
 ):
@@ -139,12 +145,16 @@
     def at_x(o):
         return ((y * nx + (x + o) % nx) * nc + c, z)
 
+    def at_y_other(o):
+        return (((y + o) % ny * nx + x) * nc + other, z)
+
     at_core = ((y * nx + x) * nc + other, z)
 
     barrier = pltpu.get_barrier_semaphore()
     peers = (
         [at_z(o) for o in offs_z]
         + [at_y(o) for o in offs_y]
+        + [at_y_other(o) for o in offs_y]
         + [at_x(o) for o in offs_x]
         + [at_core]
     )
@@ -214,7 +224,7 @@
             )
         hidden = jnp.concatenate(hidden, axis=0)
         mean = jnp.sum(hidden.reshape(lz, tokens, units), axis=1) * (1.0 / tokens)
-        pooled[pl.ds(pl.multiple_of(j * lz, lz), lz), :] = mean
+        pool_in[0, c, pl.ds(pl.multiple_of(j * lz, lz), lz), :] = mean
         rest = mean - mean.astype(BF16).astype(F32)
         both = jnp.concatenate([mean, rest], axis=0).astype(BF16)
         out = lax.dot_general(both, dnw[...], NT, preferred_element_type=F32)
@@ -237,7 +247,7 @@
         enc_copy(t).start()
         return carry
 
-    early = min(2, nz - 1)
+    early = min(5, nz - 1)
     in_copies[1].wait()
     lax.fori_loop(0, early, encode_step, 0)
     pl.semaphore_wait(barrier, len(peers))
@@ -258,18 +268,23 @@
     ]
     for copy in lv_copies:
         copy.start()
+    pool_copies = [remote(pool_in.at[0, c], pool_in.at[0, c], pool_ss.at[0], pool_rs.at[0], at_core)]
+    pool_copies += [
+        remote(pool_in.at[0, c], pool_in.at[o, c], pool_ss.at[o], pool_rs.at[o], at_x(o)) for o in offs_x
+    ]
+    for copy in pool_copies:
+        copy.start()
 
     in_copies[3].wait()
+    local = (ids[...] - lab * labels).astype(F32)
     idp[...] = jnp.full(idp.shape, -1.0, F32)
-    local = (ids[...] - lab * labels).astype(F32)
-    idp[0:192, 0:10] = local
-    idp[192:256, 0:10] = local[128:192]
-    idt[...] = jnp.transpose(idp[...])
+    idp[0:10, 0:64] = local[:, 128:192]
+    idt[...] = pltpu.roll(idp[...], 64, 1)
     lane = lax.broadcasted_iota(jnp.int32, (1, 128), 1)
     idpack[...] = jnp.full(idpack.shape, -1.0, F32)
-    idpack[0:10, :] = idt[0:10, 0:128]
+    idpack[0:10, :] = local[:, 0:128]
     for r in range(5):
-        idpack[10 + r : 11 + r, :] = jnp.where(lane < 64, idt[r : r + 1, 128:256], idt[r + 5 : r + 6, 128:256])
+        idpack[10 + r : 11 + r, :] = jnp.where(lane < 64, idp[r : r + 1, :], idt[r + 5 : r + 6, :])
 
     def owned(p, count):
         slots = lax.broadcasted_iota(jnp.int32, (count, 128), 0).astype(F32)
@@ -294,7 +309,7 @@
         text_t[:, rows] = jnp.transpose(text[rows, :])
         return carry
 
-    lax.fori_loop(0, text.shape[0] // 256, turn, 0)
+    turns = text.shape[0] // 256
     in_copies[4].wait()
     in_copies[5].wait()
 
@@ -309,22 +324,23 @@
         sc_c[p : p + 1, :] = jnp.sum(jnp.where(owned(p, labels), block, 0.0), axis=0, keepdims=True)
     score_copies = []
 
-    def exchange(src, dst, base, offs, at):
+    def exchange(src, dst, base, offs, at, first, last):
         copies = [
             remote(src, dst.at[o], sc_ss.at[base + o], sc_rs.at[base + o], at(o)) for o in offs
         ]
         score_copies.extend(copies)
         for copy in copies:
             copy.start()
+        lax.fori_loop(first, last, turn, 0)
         acc = src[...]
         for copy, o in zip(copies, offs):
             copy.wait_recv()
             acc += dst[o]
         return acc
 
-    sc_x[...] = exchange(sc_c, sc_c_in, 0, [1], lambda o: at_core)
-    sc_y[...] = exchange(sc_x, sc_x_in, 2, offs_x, at_x)
-    scores = exchange(sc_y, sc_y_in, 2 + nx, offs_y, at_y)
+    sc_x[...] = exchange(sc_c, sc_c_in, 0, [1], lambda o: at_core, 0, 0)
+    sc_y[...] = exchange(sc_x, sc_x_in, 2, offs_x, at_x, 0, turns // 4)
+    scores = exchange(sc_y, sc_y_in, 2 + nx, offs_y, at_y, turns // 4, turns)
 
     temper = 1.0 / math.sqrt(width)
     scores = scores * temper
@@ -366,16 +382,22 @@
         qt[half, 128:192, :] = terms[128:192, cols] + terms[192:256, cols]
     q_core = remote(qt.at[other], q_c_in, q_ss.at[0], q_rs.at[0], at_core)
     q_core.start()
-    qx = 192 // nx
-    owners = 6 if ny == 8 else ny
-    qy = qx // owners
+    pool_back = []
+    for copy, o in zip(pool_copies[1:], offs_x):
+        copy.wait_recv()
+        pool_back.append(
+            remote(pool_in.at[o, c], pool_in.at[o, c], pool_ss.at[nx + o], pool_rs.at[nx + o], at_core)
+        )
+        pool_back[-1].start()
+    qy = 192 // ny
+    base_x, base_g = 1 + ny, 1 + ny + nx
     q_core.wait_recv()
     q_one[...] = qt[c] + q_c_in[...]
-    q_x_copies = []
-    for o in offs_x:
-        rows = pl.ds(pl.multiple_of((x + o) % nx * qx, qx), qx)
-        q_x_copies.append(remote(q_one.at[rows], q_x_in.at[o], q_ss.at[1 + o], q_rs.at[1 + o], at_x(o)))
-        q_x_copies[-1].start()
+    q_y_copies = []
+    for o in offs_y:
+        rows = pl.ds(pl.multiple_of((y + o) % ny * qy, qy), qy)
+        q_y_copies.append(remote(q_one.at[rows], q_y_in.at[o], q_ss.at[1 + o], q_rs.at[1 + o], at_y(o)))
+        q_y_copies[-1].start()
 
     total = lg_part[own_rows, :]
     for copy, o in zip(lgr_copies, offs_z):
@@ -386,31 +408,6 @@
     for copy in lga_copies:
         copy.start()
 
-    acc = q_one[pl.ds(pl.multiple_of(x * qx, qx), qx), :]
-    for copy, o in zip(q_x_copies, offs_x):
-        copy.wait_recv()
-        acc += q_x_in[o]
-    q_two[...] = acc
-    base_y = 1 + nx
-    base_g = base_y + ny
-
-    def q_y_copy(b):
-        o = (b - y + ny) % ny
-        return o, remote(
-            q_two.at[pl.ds(b * qy, qy)],
-            q_y_in.at[o],
-            q_ss.at[base_y + b],
-            q_rs.at[base_y + o],
-            ((b * nx + x) * nc + c, z),
-        )
-
-    for b in range(owners):
-        o, copy = q_y_copy(b)
-
-        @pl.when(o != 0)
-        def _():
-            copy.start()
-
     seen = cnt[...]
     for copy, o in zip(cnt_copies, offs_z):
         copy.wait_recv()
@@ -420,21 +417,40 @@
     )
     touched = jnp.sum(jnp.where(diag, seen[0:1], 0.0), axis=1, keepdims=True) > 0.5
 
+    pool_copies[0].wait_recv()
+    for copy in pool_back:
+        copy.wait_recv()
+    for o in range(nx):
+        for k in range(nc):
+            mean = pool_in[o, k]
+            whole = mean.astype(BF16)
+            pool_bf[o, k * labels : (k + 1) * labels, :] = whole
+            pool_bf[o, (nc + k) * labels : (nc + k + 1) * labels, :] = (mean - whole.astype(F32)).astype(BF16)
+
     for copy in lga_copies:
         copy.wait_recv()
     grad = lg[...]
     out_grad = grad.astype(BF16)
     hidden_grad = jnp.dot(out_grad, dnw[...], preferred_element_type=F32) * (1.0 / tokens)
 
-    mean = pooled[...]
-    rest = mean - mean.astype(BF16).astype(F32)
-    both = jnp.concatenate([mean, rest], axis=0).astype(BF16)
-    twice = jnp.concatenate([out_grad, out_grad], axis=0)
-    down_part = lax.dot_general(twice, both, TN, preferred_element_type=F32)
-    wpart[0] = down_part.reshape(wpart.shape[1:])
-    w_core = [remote(wpart.at[k, other], w_c_in.at[k], w_ss.at[k, 0], w_rs.at[k, 0], at_core) for k in range(2)]
-    w_core[0].start()
-
+    half_rows = width // nc
+    cols_other = pl.ds(pl.multiple_of(other * half_rows, half_rows), half_rows)
+    og_core = remote(lg.at[:, cols_other], lg_pair.at[c], og_ss.at[0], og_rs.at[0], at_core)
+    og_core.start()
+
+    own_y = pl.ds(pl.multiple_of(y * qy, qy), qy)
+    acc = q_one[own_y, :]
+    for copy, o in zip(q_y_copies, offs_y):
+        copy.wait_recv()
+        acc += q_y_in[o]
+    q_x_in[x] = acc
+    q_x_copies = [
+        remote(q_x_in.at[x], q_x_in.at[x], q_ss.at[base_x + o], q_rs.at[base_x + o], at_x(o)) for o in offs_x
+    ]
+    for copy in q_x_copies:
+        copy.start()
+
+    lg_pair[c] = jnp.where(c == 0, grad[:, :half_rows], grad[:, half_rows:])
     for j in range(nz):
         rows = slice(j * rows_z, (j + 1) * rows_z)
         spreaded = jnp.broadcast_to(
@@ -442,50 +458,110 @@
         ).reshape(rows_z, units)
         pgrad[rows, :] = (slope[rows, :] * spreaded).astype(BF16)
 
-    half_rows = width // nc
-
-    def up_half(h):
-        rows = pl.ds(pl.multiple_of(h * half_rows, half_rows), half_rows)
+    og_core.wait_recv()
+    pair = lg_pair[...].reshape(nc * labels, half_rows).astype(BF16).astype(F32)
+    og_t[...] = jnp.transpose(pair).reshape(og_t.shape)
+    og_copies = []
+    for o in offs_x:
+        og_copies.append(
+            remote(og_t.at[:, (x + o) % nx], og_in.at[o], og_ss.at[1 + o], og_rs.at[1 + o], at_x(o))
+        )
+        og_copies[-1].start()
+
+    per_core = ny // nc
+    pieces = 2 if per_core % 2 == 0 else 1
+    per_piece = per_core // pieces
+    piece_rows = half_rows // pieces
+
+    def up_piece(h, p):
+        rows = pl.ds(pl.multiple_of(h * half_rows + p * piece_rows, piece_rows), piece_rows)
         part = jnp.dot(text_t[rows, :], pgrad[...], preferred_element_type=F32)
-        wpart[1, h] = part.reshape(wpart.shape[2:])
-
-    up_half(other)
-    w_core[1].start()
-
-    w_x_copies = [[], []]
-
-    def across_x(k):
-        w_core[k].wait_recv()
-        w_one[k] = wpart[k, c] + w_c_in[k]
+        upart[h, p] = part.reshape(upart.shape[2:])
+
+    u_core = []
+    for p in range(pieces):
+        up_piece(other, p)
+        u_core.append(remote(upart.at[other, p], u_c_in.at[p], u_ss.at[p, 0], u_rs.at[p, 0], at_core))
+        u_core[p].start()
+
+    u_x_copies = [[], []]
+
+    def across_x(p):
+        u_core[p].wait_recv()
+        u_one[p] = upart[c, p] + u_c_in[p]
         for o in offs_x:
             copy = remote(
-                w_one.at[k, :, (x + o) % nx],
-                w_x_in.at[k, o],
-                w_ss.at[k, 1 + o],
-                w_rs.at[k, 1 + o],
+                u_one.at[p, :, (x + o) % nx],
+                u_x_in.at[p, o],
+                u_ss.at[p, 1 + o],
+                u_rs.at[p, 1 + o],
                 at_x(o),
             )
             copy.start()
-            w_x_copies[k].append(copy)
-
-    across_x(0)
-    up_half(c)
-    across_x(1)
-
-    @pl.when(y < owners)
-    def _():
-        acc = q_two[pl.ds(pl.multiple_of(y % owners * qy, qy), qy), :]
-        for o in offs_y:
-            remote(
-                q_two.at[pl.ds(0, qy)], q_y_in.at[o], q_ss.at[base_y], q_rs.at[base_y + o], at_y(o)
-            ).wait_recv()
-            acc += q_y_in[o]
-        mine = pl.ds(pl.multiple_of(y % owners * qy, qy), qy)
-        q_four[mine, :] = acc
-        for o in offs_y:
-            remote(
-                q_four.at[mine], q_four.at[mine], q_ss.at[base_g + o], q_rs.at[base_g + y], at_y(o)
-            ).start()
+            u_x_copies[p].append(copy)
+
+    for p in range(pieces):
+        up_piece(c, p)
+        across_x(p)
+
+    rows_out = w_out.shape[1]
+    step_rows, slice_rows = rows_out // 8 * 8, -(-rows_out // 8) * 8
+
+    def w_y_copies(k, b):
+        goal = c * per_core + b
+        o = (goal - y + ny) % ny
+        copies = []
+        for side, core in enumerate((c, other)):
+            rows = pl.ds(pl.multiple_of(core * step_rows, 8), slice_rows)
+            copies.append(
+                remote(
+                    w_two.at[k, b, rows],
+                    w_y_in.at[k, o],
+                    w_ss.at[k, side, b],
+                    w_rs.at[k, o],
+                    ((goal * nx + x) * nc + core, z),
+                )
+            )
+        return o, copies
+
+    def across_y(k, b):
+        o, copies = w_y_copies(k, b)
+        copies[1].start()
+
+        @pl.when(o != 0)
+        def _():
+            copies[0].start()
+
+        @pl.when(o == 0)
+        def _():
+            w_y_in[k, 0] = w_two[k, b, pl.ds(pl.multiple_of(c * step_rows, 8), slice_rows), :]
+
+    def down_term(values, o):
+        values = values.reshape(half_rows // nx, nc * labels).astype(BF16)
+        return jnp.dot(
+            jnp.concatenate([values, values], axis=1), pool_bf[o], preferred_element_type=F32
+        )
+
+    acc = down_term(og_t[:, x], 0)
+    for copy, o in zip(og_copies, offs_x):
+        copy.wait_recv()
+        acc += down_term(og_in[o], o)
+    w_two[0] = acc.reshape(w_two.shape[1:])
+    for b in range(per_core):
+        across_y(0, b)
+
+    for copy in q_x_copies:
+        copy.wait_recv()
+    acc = q_x_in[0]
+    for i in range(1, nx):
+        acc += q_x_in[i]
+    q_five[own_y, :] = acc
+    q_g_copies = [
+        remote(q_five.at[own_y], q_five.at[own_y], q_ss.at[base_g + o], q_rs.at[base_g + o], at_y(o))
+        for o in offs_y
+    ]
+    for copy in q_g_copies:
+        copy.start()
 
     in_copies[6].wait()
     in_copies[7].wait()
@@ -502,80 +578,41 @@
     for copy in out_copies:
         copy.start()
 
-    for b in range(owners):
-
-        @pl.when(y != b)
+    for p in range(pieces):
+        acc = u_one[p, :, x]
+        for copy, o in zip(u_x_copies[p], offs_x):
+            copy.wait_recv()
+            acc += u_x_in[p, o]
+        for i in range(per_piece):
+            w_two[1, p * per_piece + i] = acc[i]
+            across_y(1, p * per_piece + i)
+
+    for copy in q_g_copies:
+        copy.wait_recv()
+    q_back = remote(q_five, q_six, q_ss.at[base_g], q_rs.at[base_g], at_core)
+    q_back.start()
+
+    holder = y // per_core == c
+
+    def last(k):
+        @pl.when(jnp.logical_not(holder))
         def _():
-            rows = pl.ds(b * qy, qy)
             remote(
-                q_four.at[rows], q_four.at[rows], q_ss.at[base_g], q_rs.at[base_g + b], at_core
+                w_two.at[k, 0, pl.ds(0, slice_rows)], w_y_in.at[k, 0], w_ss.at[k, 0, 0], w_rs.at[k, 0], at_core
             ).wait_recv()
 
-    own_x = pl.ds(pl.multiple_of(x * qx, qx), qx)
-    q_five[own_x, :] = q_four[...]
-    base_h = base_g + ny
-    q_xg_copies = [
-        remote(q_four, q_five.at[own_x], q_ss.at[base_h + o], q_rs.at[base_h + o], at_x(o)) for o in offs_x
-    ]
-    for copy in q_xg_copies:
-        copy.start()
-
-    per_core = ny // nc
-
-    def w_y_copy(k, b):
-        goal = c * per_core + b
-        o = (goal - y + ny) % ny
-        return o, remote(
-            w_two.at[k, b],
-            w_y_in.at[k, o],
-            w_ss.at[k, 1 + nx + b],
-            w_rs.at[k, 1 + nx + o],
-            ((goal * nx + x) * nc + c, z),
-        )
-
-    def across_y(k):
-        acc = w_one[k, :, x]
-        for copy, o in zip(w_x_copies[k], offs_x):
-            copy.wait_recv()
-            acc += w_x_in[k, o]
-        w_two[k] = acc
-        for b in range(per_core):
-            o, copy = w_y_copy(k, b)
-
-            @pl.when(o != 0)
-            def _():
-                copy.start()
-
-    across_y(0)
-    across_y(1)
-
-    for copy in q_xg_copies:
-        copy.wait_recv()
-    q_back = remote(q_five, q_six, q_ss.at[base_h + nx], q_rs.at[base_h + nx], at_core)
-    q_back.start()
-
-    holder = y // per_core == c
-    rows_out = w_out.shape[1]
-
-    def w_last(k):
-        return remote(
-            w_give.at[k], w_got.at[k], w_ss.at[k, 1 + nx + ny], w_rs.at[k, 1 + nx + ny], at_core
-        )
-
-    for k in range(2):
-
-        @pl.when(holder)
-        def _():
-            acc = w_two[k, y % per_core]
-            for o in offs_y:
-                remote(
-                    w_two.at[k, 0], w_y_in.at[k, o], w_ss.at[k, 0], w_rs.at[k, 1 + nx + o], at_y(o)
-                ).wait_recv()
-                acc += w_y_in[k, o]
-            first, last = acc[:rows_out], acc[rows_out:]
-            w_give[k, 0:rows_out, :] = jnp.where(c == 0, last, first)
-            w_last(k).start()
-            w_out[k] = jnp.where(c == 0, first, last)
+        for o in offs_y:
+            remote(
+                w_two.at[k, 0, pl.ds(0, slice_rows)], w_y_in.at[k, o], w_ss.at[k, 0, 0], w_rs.at[k, o], at_y(o)
+            ).wait_recv()
+        acc = w_y_in[k, 0]
+        for o in range(1, ny):
+            acc += w_y_in[k, o]
+        shift = rows_out - step_rows
+        w_out[k] = jnp.where(c == 0, acc[:rows_out], acc[shift : shift + rows_out])
+        pltpu.make_async_copy(w_out.at[k], (down_o, up_o)[k], out_sem.at[5 + k]).start()
+
+    last(0)
 
     for half in range(2):
         cols = slice(half * (width // 2), (half + 1) * (width // 2))
@@ -592,56 +629,29 @@
         def _():
             pltpu.make_async_copy(q_six, query_o.at[:, cols], out_sem.at[4]).start()
 
-    for k in range(2):
-
-        @pl.when(jnp.logical_not(holder))
-        def _():
-            w_last(k).wait_recv()
-            w_out[k] = w_got[k, 0:rows_out, :]
-
-    w_writes = [
-        pltpu.make_async_copy(w_out.at[0], down_o, out_sem.at[5]),
-        pltpu.make_async_copy(w_out.at[1], up_o, out_sem.at[6]),
-    ]
-    for copy in w_writes:
-        copy.start()
+    last(1)
 
     for o in offs_z:
         remote(enc.at[o], enc_in.at[o], enc_ss.at[o], enc_rs.at[o], at_z(o)).wait_send()
     for copy in (
-        lv_copies + cnt_copies + score_copies + lgr_copies + lga_copies + q_x_copies + q_xg_copies
-        + w_core + w_x_copies[0] + w_x_copies[1] + [q_core, q_back]
+        lv_copies + cnt_copies + score_copies + pool_copies + pool_back + lgr_copies + lga_copies
+        + q_y_copies + q_x_copies + q_g_copies + og_copies + u_core + u_x_copies[0] + u_x_copies[1]
+        + [q_core, q_back, og_core]
     ):
         copy.wait_send()
-    for b in range(owners):
-        o, copy = q_y_copy(b)
-
-        @pl.when(o != 0)
-        def _():
-            copy.wait_send()
-
-    @pl.when(y < owners)
-    def _():
-        mine = pl.ds(pl.multiple_of(y % owners * qy, qy), qy)
-        for o in offs_y:
-            remote(
-                q_four.at[mine], q_four.at[mine], q_ss.at[base_g + o], q_rs.at[base_g + y], at_y(o)
-            ).wait_send()
-
     for k in range(2):
         for b in range(per_core):
-            o, copy = w_y_copy(k, b)
+            o, copies = w_y_copies(k, b)
+            copies[1].wait_send()
 
             @pl.when(o != 0)
             def _():
-                copy.wait_send()
-
-        @pl.when(holder)
-        def _():
-            w_last(k).wait_send()
-
-    for copy in out_copies + w_writes:
+                copies[0].wait_send()
+
+    for copy in out_copies:
         copy.wait()
+    pltpu.make_async_copy(w_out.at[0], down_o, out_sem.at[5]).wait()
+    pltpu.make_async_copy(w_out.at[1], up_o, out_sem.at[6]).wait()
     pltpu.make_async_copy(q_five, query_o.at[:, 0 : width // 2], out_sem.at[3]).wait()
     pltpu.make_async_copy(q_six, query_o.at[:, 0 : width // 2], out_sem.at[4]).wait()
 
@@ -657,8 +667,9 @@
     chip_rows = rows_out * nc
     per_core = ny // nc
     half = width // 2
-    qx = 192 // nx
-    qy = qx // (6 if ny == 8 else ny)
+    qy = 192 // ny
+    pieces = 2 if per_core % 2 == 0 else 1
+    per_piece = per_core // pieces
     staged = -(-rows_out // 8) * 8
     vmem = pltpu.VMEM
     dma = pltpu.SemaphoreType.DMA
@@ -668,18 +679,19 @@
         vmem((width, units), BF16),
         vmem((width, units), BF16),
         vmem((256, width), BF16),
-        vmem((192, 10), jnp.int32),
+        vmem((10, 192), jnp.int32),
         vmem((labels, width), F32),
         vmem((labels, width), F32),
         vmem((labels, width), F32),
         vmem((rows, units), F32),
-        vmem((labels, units), F32),
+        vmem((nx, nc, labels, units), F32),
+        vmem((nx, 2 * nc * labels, units), BF16),
         vmem((nz, lz, width), F32),
         vmem((nz, lz, width), F32),
         vmem((labels, width), F32),
         vmem((labels, width), BF16),
-        vmem((256, 128), F32),
-        vmem((128, 256), F32),
+        vmem((16, 128), F32),
+        vmem((16, 128), F32),
         vmem((16, 128), F32),
         vmem((8, 128), F32),
         vmem((nz, 8, 128), F32),
@@ -695,21 +707,20 @@
         vmem((2, 192, half), F32),
         vmem((192, half), F32),
         vmem((192, half), F32),
-        vmem((nx, qx, half), F32),
-        vmem((qx, half), F32),
         vmem((ny, qy, half), F32),
-        vmem((qx, half), F32),
+        vmem((nx, qy, half), F32),
         vmem((192, half), F32),
         vmem((192, half), F32),
+        vmem((nc, labels, half), F32),
+        vmem((per_core, nx, chip_rows, nc * labels), F32),
+        vmem((nx, per_core, chip_rows, nc * labels), F32),
         vmem((rows, units), BF16),
-        vmem((2, nc, per_core, nx, chip_rows, units), F32),
-        vmem((2, per_core, nx, chip_rows, units), F32),
-        vmem((2, per_core, nx, chip_rows, units), F32),
-        vmem((2, nx, per_core, chip_rows, units), F32),
+        vmem((nc, pieces, per_piece, nx, chip_rows, units), F32),
+        vmem((pieces, per_piece, nx, chip_rows, units), F32),
+        vmem((pieces, per_piece, nx, chip_rows, units), F32),
+        vmem((pieces, nx, per_piece, chip_rows, units), F32),
         vmem((2, per_core, chip_rows, units), F32),
-        vmem((2, ny, chip_rows, units), F32),
-        vmem((2, staged, units), F32),
-        vmem((2, staged, units), F32),
+        vmem((2, ny, staged, units), F32),
         vmem((2, rows_out, units), F32),
         vmem((labels, width), F32),
         vmem((labels, width), F32),
@@ -729,14 +740,20 @@
         dma((nz,)),
         dma((nz,)),
         dma((nz,)),
-        dma((2 + 2 * nx + 2 * ny,)),
-        dma((2 + 2 * nx + 2 * ny,)),
-        dma((2, 2 + nx + ny)),
-        dma((2, 2 + nx + ny)),
+        dma((1 + nx + 2 * ny,)),
+        dma((1 + nx + 2 * ny,)),
+        dma((2 * nx,)),
+        dma((2 * nx,)),
+        dma((1 + nx,)),
+        dma((1 + nx,)),
+        dma((pieces, 1 + nx)),
+        dma((pieces, 1 + nx)),
+        dma((2, 2, per_core)),
+        dma((2, ny)),
     ]
     hbm = pl.BlockSpec(memory_space=pl.ANY)
     flops = 2 * rows * width * units * 2
-    return pl.pallas_call(
+    results = pl.pallas_call(
         functools.partial(kernel, dims),
         out_shape=[
             jax.ShapeDtypeStruct((labels, width), F32),
@@ -754,7 +771,31 @@
         compiler_params=pltpu.CompilerParams(
             collective_id=0, has_side_effects=True, vmem_limit_bytes=56 * 2**20
         ),
-    )(queries, label_ids, text_rows, up_weight, down_weight, free_vectors, moments, seconds)
+    )(queries, label_ids.T, text_rows, up_weight, down_weight, free_vectors, moments, seconds)
+    count = len(results)
+    return pl.pallas_call(
+        hand_over,
+        out_shape=[jax.ShapeDtypeStruct(r.shape, r.dtype) for r in results],
+        in_specs=[hbm] * count,
+        out_specs=[hbm] * count,
+        scratch_shapes=[vmem(r.shape, r.dtype) for r in results] + [dma((count,)), dma((count,))],
+        name="hand_over",
+    )(*results)
+
+
+def hand_over(*refs):
+    count = (len(refs) - 2) // 3
+    loads = [pltpu.make_async_copy(refs[i], refs[2 * count + i], refs[-2].at[i]) for i in range(count)]
+    stores = [
+        pltpu.make_async_copy(refs[2 * count + i], refs[count + i], refs[-1].at[i]) for i in range(count)
+    ]
+    for copy in loads:
+        copy.start()
+    for load, store in zip(loads, stores):
+        load.wait()
+        store.start()
+    for copy in stores:
+        copy.wait()
 
 
 def build(mesh, dims):

time: 88.6 us -> 80.7 us (0.911)
  local copies, waits for them, and re-layouts: 10.9 us -> 0 us
  Pallas kernels: 76.7 us -> 79.9 us
    unnamed x7 -> x0, local copies, waits for them, and re-layouts: 10.9 us -> none
    pallas_call x0 -> x1, Pallas kernels: none -> 2.28 us  [body(): pl.pallas_call(hand_over, out_shape=[jax.ShapeDtypeStruct(r.shape, r.dtyp...]
    pallas_call x1, Pallas kernels: 76.7 us -> 77.6 us  [body(): pl.pallas_call(functools.partial(kernel, dims), out_shape=[jax.ShapeDtype...]
where the time goes in v2:
time: 80.7 us; the launch traced here: 80.5 us
  Pallas kernels  79.9 us (99%)
    pallas_call x1, Pallas kernels, body(): pl.pallas_call(functools.partial(kernel, dims), out_shape=[jax.ShapeDtype...  77.6 us
    pallas_call x1, Pallas kernels, body(): pl.pallas_call(hand_over, out_shape=[jax.ShapeDtypeStruct(r.shape, r.dtyp...  2.28 us

profile of v2, /device:TPU:1, one launch (start us, length us, event | category | flops | bytes accessed | tf_op | source)
XLA Modules:
  0.0 80.5 jit_solution(16147702732704316382)
XLA Ops:
  0.6 77.6 %step.1 = (f32[64,768]{1,0:T(8,128)}, f32[64,768]{1,0:T(8,128)}, f32[64,768]{1,0:T(8,128)}, f32[192,768]{1,0:T(8,128)}, f32[12,384]{1,0:T(8,128)}, /*index=5*/f32[12,384]{1,0:T(8,128)}) custom-call(bf16[192,768]{1,0:T(8,128)(2,1)} %queries_h.1, s32[10,192]{1,0:T(8,128)} %bitcast.3, bf16[2048,768]{1,0:T(8,128)(2,1)} %bitcast.2, bf16[768,384]{1,0:T(8,128)(2,1)} %up_h.1, ...), custom_call_target="tpu_custom_call" | custom-call | flops 2415919104 | bytes 8388608 | tf_op jit(solution)/shard_map/step/pallas_call | solution.py:756
  78.3 2.3 %hand_over.1 = (f32[64,768]{1,0:T(8,128)}, f32[64,768]{1,0:T(8,128)}, f32[64,768]{1,0:T(8,128)}, f32[192,768]{1,0:T(8,128)}, f32[12,384]{1,0:T(8,128)}, /*index=5*/f32[12,384]{1,0:T(8,128)}) custom-call(f32[64,768]{1,0:T(8,128)} %get-tuple-element.12.refs_0_, f32[64,768]{1,0:T(8,128)} %get-tuple-element.13.refs_1_, f32[64,768]{1,0:T(8,128)} %get-tuple-element.14.refs_2_, ...), custom_call_target="tpu_custom_call" | custom-call | tf_op jit(solution)/shard_map/hand_over/pallas_call | solution.py:776

commit v3 on v2

--- a/solution.py
+++ b/solution.py
@@ -78,8 +78,10 @@
     qt,
     q_c_in,
     q_one,
+    q_x_in,
+    q_two,
     q_y_in,
-    q_x_in,
+    q_four,
     q_five,
     q_six,
     lg_pair,
@@ -247,7 +249,7 @@
         enc_copy(t).start()
         return carry
 
-    early = min(5, nz - 1)
+    early = min(2, nz - 1)
     in_copies[1].wait()
     lax.fori_loop(0, early, encode_step, 0)
     pl.semaphore_wait(barrier, len(peers))
@@ -313,6 +315,7 @@
     in_copies[4].wait()
     in_copies[5].wait()
 
+    lax.fori_loop(0, turns * 3 // 8, turn, 0)
     for copy in lv_copies:
         copy.wait_recv()
     lbf[...] = lvec[...].astype(BF16)
@@ -339,8 +342,8 @@
         return acc
 
     sc_x[...] = exchange(sc_c, sc_c_in, 0, [1], lambda o: at_core, 0, 0)
-    sc_y[...] = exchange(sc_x, sc_x_in, 2, offs_x, at_x, 0, turns // 4)
-    scores = exchange(sc_y, sc_y_in, 2 + nx, offs_y, at_y, turns // 4, turns)
+    sc_y[...] = exchange(sc_x, sc_x_in, 2, offs_x, at_x, turns * 3 // 8, turns * 5 // 8)
+    scores = exchange(sc_y, sc_y_in, 2 + nx, offs_y, at_y, turns * 5 // 8, turns)
 
     temper = 1.0 / math.sqrt(width)
     scores = scores * temper
@@ -389,15 +392,17 @@
             remote(pool_in.at[o, c], pool_in.at[o, c], pool_ss.at[nx + o], pool_rs.at[nx + o], at_core)
         )
         pool_back[-1].start()
-    qy = 192 // ny
-    base_x, base_g = 1 + ny, 1 + ny + nx
+    qx = 192 // nx
+    owners = 6 if ny == 8 else ny
+    qy = qx // owners
+    base_y, base_g, base_h = 1 + nx, 1 + nx + ny, 1 + nx + 2 * ny
     q_core.wait_recv()
     q_one[...] = qt[c] + q_c_in[...]
-    q_y_copies = []
-    for o in offs_y:
-        rows = pl.ds(pl.multiple_of((y + o) % ny * qy, qy), qy)
-        q_y_copies.append(remote(q_one.at[rows], q_y_in.at[o], q_ss.at[1 + o], q_rs.at[1 + o], at_y(o)))
-        q_y_copies[-1].start()
+    q_x_copies = []
+    for o in offs_x:
+        rows = pl.ds(pl.multiple_of((x + o) % nx * qx, qx), qx)
+        q_x_copies.append(remote(q_one.at[rows], q_x_in.at[o], q_ss.at[1 + o], q_rs.at[1 + o], at_x(o)))
+        q_x_copies[-1].start()
 
     total = lg_part[own_rows, :]
     for copy, o in zip(lgr_copies, offs_z):
@@ -416,6 +421,30 @@
         jnp.int32, (labels, 128), 1
     )
     touched = jnp.sum(jnp.where(diag, seen[0:1], 0.0), axis=1, keepdims=True) > 0.5
+
+    own_x = pl.ds(pl.multiple_of(x * qx, qx), qx)
+    acc = q_one[own_x, :]
+    for copy, o in zip(q_x_copies, offs_x):
+        copy.wait_recv()
+        acc += q_x_in[o]
+    q_two[...] = acc
+
+    def q_y_copy(b):
+        o = (b - y + ny) % ny
+        return o, remote(
+            q_two.at[pl.ds(b * qy, qy)],
+            q_y_in.at[o],
+            q_ss.at[base_y + b],
+            q_rs.at[base_y + o],
+            ((b * nx + x) * nc + c, z),
+        )
+
+    for b in range(owners):
+        o, q_copy = q_y_copy(b)
+
+        @pl.when(o != 0)
+        def _():
+            q_copy.start()
 
     pool_copies[0].wait_recv()
     for copy in pool_back:
@@ -438,18 +467,6 @@
     og_core = remote(lg.at[:, cols_other], lg_pair.at[c], og_ss.at[0], og_rs.at[0], at_core)
     og_core.start()
 
-    own_y = pl.ds(pl.multiple_of(y * qy, qy), qy)
-    acc = q_one[own_y, :]
-    for copy, o in zip(q_y_copies, offs_y):
-        copy.wait_recv()
-        acc += q_y_in[o]
-    q_x_in[x] = acc
-    q_x_copies = [
-        remote(q_x_in.at[x], q_x_in.at[x], q_ss.at[base_x + o], q_rs.at[base_x + o], at_x(o)) for o in offs_x
-    ]
-    for copy in q_x_copies:
-        copy.start()
-
     lg_pair[c] = jnp.where(c == 0, grad[:, :half_rows], grad[:, half_rows:])
     for j in range(nz):
         rows = slice(j * rows_z, (j + 1) * rows_z)
@@ -467,6 +484,24 @@
             remote(og_t.at[:, (x + o) % nx], og_in.at[o], og_ss.at[1 + o], og_rs.at[1 + o], at_x(o))
         )
         og_copies[-1].start()
+
+    mine = pl.ds(pl.multiple_of(y % owners * qy, qy), qy)
+    q_g_copies = [
+        remote(q_four.at[mine], q_four.at[mine], q_ss.at[base_g + o], q_rs.at[base_g + y], at_y(o))
+        for o in offs_y
+    ]
+
+    @pl.when(y < owners)
+    def _():
+        acc = q_two[mine, :]
+        for o in offs_y:
+            remote(
+                q_two.at[pl.ds(0, qy)], q_y_in.at[o], q_ss.at[base_y], q_rs.at[base_y + o], at_y(o)
+            ).wait_recv()
+            acc += q_y_in[o]
+        q_four[mine, :] = acc
+        for copy in q_g_copies:
+            copy.start()
 
     per_core = ny // nc
     pieces = 2 if per_core % 2 == 0 else 1
@@ -550,17 +585,20 @@
     for b in range(per_core):
         across_y(0, b)
 
-    for copy in q_x_copies:
-        copy.wait_recv()
-    acc = q_x_in[0]
-    for i in range(1, nx):
-        acc += q_x_in[i]
-    q_five[own_y, :] = acc
-    q_g_copies = [
-        remote(q_five.at[own_y], q_five.at[own_y], q_ss.at[base_g + o], q_rs.at[base_g + o], at_y(o))
-        for o in offs_y
+    for b in range(owners):
+
+        @pl.when(y != b)
+        def _():
+            rows = pl.ds(b * qy, qy)
+            remote(
+                q_four.at[rows], q_four.at[rows], q_ss.at[base_g], q_rs.at[base_g + b], at_core
+            ).wait_recv()
+
+    q_five[own_x, :] = q_four[...]
+    q_h_copies = [
+        remote(q_four, q_five.at[own_x], q_ss.at[base_h + o], q_rs.at[base_h + o], at_x(o)) for o in offs_x
     ]
-    for copy in q_g_copies:
+    for copy in q_h_copies:
         copy.start()
 
     in_copies[6].wait()
@@ -587,9 +625,9 @@
             w_two[1, p * per_piece + i] = acc[i]
             across_y(1, p * per_piece + i)
 
-    for copy in q_g_copies:
+    for copy in q_h_copies:
         copy.wait_recv()
-    q_back = remote(q_five, q_six, q_ss.at[base_g], q_rs.at[base_g], at_core)
+    q_back = remote(q_five, q_six, q_ss.at[base_h], q_rs.at[base_h], at_core)
     q_back.start()
 
     holder = y // per_core == c
@@ -635,10 +673,22 @@
         remote(enc.at[o], enc_in.at[o], enc_ss.at[o], enc_rs.at[o], at_z(o)).wait_send()
     for copy in (
         lv_copies + cnt_copies + score_copies + pool_copies + pool_back + lgr_copies + lga_copies
-        + q_y_copies + q_x_copies + q_g_copies + og_copies + u_core + u_x_copies[0] + u_x_copies[1]
+        + q_x_copies + q_h_copies + og_copies + u_core + u_x_copies[0] + u_x_copies[1]
         + [q_core, q_back, og_core]
     ):
         copy.wait_send()
+    for b in range(owners):
+        o, q_copy = q_y_copy(b)
+
+        @pl.when(o != 0)
+        def _():
+            q_copy.wait_send()
+
+    @pl.when(y < owners)
+    def _():
+        for copy in q_g_copies:
+            copy.wait_send()
+
     for k in range(2):
         for b in range(per_core):
             o, copies = w_y_copies(k, b)
@@ -667,7 +717,8 @@
     chip_rows = rows_out * nc
     per_core = ny // nc
     half = width // 2
-    qy = 192 // ny
+    qx = 192 // nx
+    qy = qx // (6 if ny == 8 else ny)
     pieces = 2 if per_core % 2 == 0 else 1
     per_piece = per_core // pieces
     staged = -(-rows_out // 8) * 8
@@ -707,8 +758,10 @@
         vmem((2, 192, half), F32),
         vmem((192, half), F32),
         vmem((192, half), F32),
+        vmem((nx, qx, half), F32),
+        vmem((qx, half), F32),
         vmem((ny, qy, half), F32),
-        vmem((nx, qy, half), F32),
+        vmem((qx, half), F32),
         vmem((192, half), F32),
         vmem((192, half), F32),
         vmem((nc, labels, half), F32),
@@ -740,8 +793,8 @@
         dma((nz,)),
         dma((nz,)),
         dma((nz,)),
-        dma((1 + nx + 2 * ny,)),
-        dma((1 + nx + 2 * ny,)),
+        dma((1 + 2 * nx + 2 * ny,)),
+        dma((1 + 2 * nx + 2 * ny,)),
         dma((2 * nx,)),
         dma((2 * nx,)),
         dma((1 + nx,)),

time: 80.7 us -> 73.6 us (0.912)
  Pallas kernels: 79.9 us -> 72.4 us
    pallas_call x1, Pallas kernels: 77.6 us -> 70.1 us  [body(): pl.pallas_call(functools.partial(kernel, dims), out_shape=[jax.ShapeDtype...]
where the time goes in v3:
time: 73.6 us; the launch traced here: 73 us
  Pallas kernels  72.4 us (98%)
    pallas_call x1, Pallas kernels, body(): pl.pallas_call(functools.partial(kernel, dims), out_shape=[jax.ShapeDtype...  70.1 us
    pallas_call x1, Pallas kernels, body(): pl.pallas_call(hand_over, out_shape=[jax.ShapeDtypeStruct(r.shape, r.dtyp...  2.28 us

profile of v3, /device:TPU:1, one launch (start us, length us, event | category | flops | bytes accessed | tf_op | source)
XLA Modules:
  0.0 73.0 jit_solution(16412086523057094896)
XLA Ops:
  0.6 70.1 %step.1 = (f32[64,768]{1,0:T(8,128)}, f32[64,768]{1,0:T(8,128)}, f32[64,768]{1,0:T(8,128)}, f32[192,768]{1,0:T(8,128)}, f32[12,384]{1,0:T(8,128)}, /*index=5*/f32[12,384]{1,0:T(8,128)}) custom-call(bf16[192,768]{1,0:T(8,128)(2,1)} %queries_h.1, s32[10,192]{1,0:T(8,128)} %bitcast.3, bf16[2048,768]{1,0:T(8,128)(2,1)} %bitcast.2, bf16[768,384]{1,0:T(8,128)(2,1)} %up_h.1, ...), custom_call_target="tpu_custom_call" | custom-call | flops 2415919104 | bytes 8388608 | tf_op jit(solution)/shard_map/step/pallas_call | solution.py:809
  70.7 2.3 %hand_over.1 = (f32[64,768]{1,0:T(8,128)}, f32[64,768]{1,0:T(8,128)}, f32[64,768]{1,0:T(8,128)}, f32[192,768]{1,0:T(8,128)}, f32[12,384]{1,0:T(8,128)}, /*index=5*/f32[12,384]{1,0:T(8,128)}) custom-call(f32[64,768]{1,0:T(8,128)} %get-tuple-element.12.refs_0_, f32[64,768]{1,0:T(8,128)} %get-tuple-element.13.refs_1_, f32[64,768]{1,0:T(8,128)} %get-tuple-element.14.refs_2_, ...), custom_call_target="tpu_custom_call" | custom-call | tf_op jit(solution)/shard_map/hand_over/pallas_call | solution.py:829

commit v4 on v3

--- a/solution.py
+++ b/solution.py
@@ -809,15 +809,15 @@
     results = pl.pallas_call(
         functools.partial(kernel, dims),
         out_shape=[
-            jax.ShapeDtypeStruct((labels, width), F32),
-            jax.ShapeDtypeStruct((labels, width), F32),
-            jax.ShapeDtypeStruct((labels, width), F32),
-            jax.ShapeDtypeStruct((192, width), F32),
-            jax.ShapeDtypeStruct((rows_out, units), F32),
-            jax.ShapeDtypeStruct((rows_out, units), F32),
+            pltpu.VMEM((labels, width), F32),
+            pltpu.VMEM((labels, width), F32),
+            pltpu.VMEM((labels, width), F32),
+            pltpu.VMEM((192, width), F32),
+            pltpu.VMEM((rows_out, units), F32),
+            pltpu.VMEM((rows_out, units), F32),
         ],
         in_specs=[hbm] * 8,
-        out_specs=[hbm] * 6,
+        out_specs=[pl.BlockSpec(memory_space=pltpu.VMEM)] * 6,
         scratch_shapes=scratch,
         name="step",
         cost_estimate=pl.CostEstimate(flops=flops, bytes_accessed=8 * 2**20, transcendentals=rows * units),
@@ -829,25 +829,19 @@
     return pl.pallas_call(
         hand_over,
         out_shape=[jax.ShapeDtypeStruct(r.shape, r.dtype) for r in results],
-        in_specs=[hbm] * count,
+        in_specs=[pl.BlockSpec(memory_space=pltpu.VMEM)] * count,
         out_specs=[hbm] * count,
-        scratch_shapes=[vmem(r.shape, r.dtype) for r in results] + [dma((count,)), dma((count,))],
+        scratch_shapes=[dma((count,))],
         name="hand_over",
-    )(*results)
+    )(*[pltpu.with_memory_space_constraint(r, pltpu.VMEM) for r in results])
 
 
 def hand_over(*refs):
-    count = (len(refs) - 2) // 3
-    loads = [pltpu.make_async_copy(refs[i], refs[2 * count + i], refs[-2].at[i]) for i in range(count)]
-    stores = [
-        pltpu.make_async_copy(refs[2 * count + i], refs[count + i], refs[-1].at[i]) for i in range(count)
-    ]
-    for copy in loads:
+    count = (len(refs) - 1) // 2
+    copies = [pltpu.make_async_copy(refs[i], refs[count + i], refs[-1].at[i]) for i in range(count)]
+    for copy in copies:
         copy.start()
-    for load, store in zip(loads, stores):
-        load.wait()
-        store.start()
-    for copy in stores:
+    for copy in copies:
         copy.wait()
 
 

time: 73.6 us -> 71.9 us (0.977)
  Pallas kernels: 72.4 us -> 70.7 us
    pallas_call x1, Pallas kernels: 2.28 us -> 1.07 us  [body(): pl.pallas_call(hand_over, out_shape=[jax.ShapeDtypeStruct(r.shape, r.dtyp...]
where the time goes in v4:
time: 71.9 us; the launch traced here: 71.3 us
  Pallas kernels  70.7 us (98%)
    pallas_call x1, Pallas kernels, body(): pl.pallas_call(functools.partial(kernel, dims), out_shape=[pltpu.VMEM((la...  69.6 us

profile of v4, /device:TPU:1, one launch (start us, length us, event | category | flops | bytes accessed | tf_op | source)
XLA Modules:
  0.0 71.3 jit_solution(5967264737484417014)
XLA Ops:
  0.6 69.6 %step.1 = (f32[64,768]{1,0:T(8,128)S(1)}, f32[64,768]{1,0:T(8,128)S(1)}, f32[64,768]{1,0:T(8,128)S(1)}, f32[192,768]{1,0:T(8,128)S(1)}, f32[12,384]{1,0:T(8,128)S(1)}, /*index=5*/f32[12,384]{1,0:T(8,128)S(1)}) custom-call(bf16[192,768]{1,0:T(8,128)(2,1)} %queries_h.1, s32[10,192]{1,0:T(8,128)} %bitcast.3, bf16[2048,768]{1,0:T(8,128)(2,1)} %bitcast.2, ...), custom_call_target="tpu_custom_call" | custom-call | flops 2415919104 | bytes 8388608 | tf_op jit(solution)/shard_map/step/pallas_call | solution.py:809
  70.2 1.1 %hand_over.1 = (f32[64,768]{1,0:T(8,128)}, f32[64,768]{1,0:T(8,128)}, f32[64,768]{1,0:T(8,128)}, f32[192,768]{1,0:T(8,128)}, f32[12,384]{1,0:T(8,128)}, /*index=5*/f32[12,384]{1,0:T(8,128)}) custom-call(f32[64,768]{1,0:T(8,128)S(1)} %get-tuple-element.12.refs_0_, f32[64,768]{1,0:T(8,128)S(1)} %get-tuple-element.13.refs_1_, ...), custom_call_target="tpu_custom_call" | custom-call | tf_op jit(solution)/shard_map/hand_over/pallas_call | solution.py:829

commit v5 on v4

--- a/solution.py
+++ b/solution.py
@@ -601,6 +601,17 @@
     for copy in q_h_copies:
         copy.start()
 
+    def up_across_y(p):
+        acc = u_one[p, :, x]
+        for copy, o in zip(u_x_copies[p], offs_x):
+            copy.wait_recv()
+            acc += u_x_in[p, o]
+        for i in range(per_piece):
+            w_two[1, p * per_piece + i] = acc[i]
+            across_y(1, p * per_piece + i)
+
+    up_across_y(0)
+
     in_copies[6].wait()
     in_copies[7].wait()
     moment = beta_one * mom[...] + (1.0 - beta_one) * grad
@@ -616,14 +627,8 @@
     for copy in out_copies:
         copy.start()
 
-    for p in range(pieces):
-        acc = u_one[p, :, x]
-        for copy, o in zip(u_x_copies[p], offs_x):
-            copy.wait_recv()
-            acc += u_x_in[p, o]
-        for i in range(per_piece):
-            w_two[1, p * per_piece + i] = acc[i]
-            across_y(1, p * per_piece + i)
+    for p in range(1, pieces):
+        up_across_y(p)
 
     for copy in q_h_copies:
         copy.wait_recv()

time: 71.9 us -> 71.9 us (level)
  no operation moved by 1% of the time
where the time goes in v5:
time: 71.9 us; the launch traced here: 71.3 us
  Pallas kernels  70.7 us (98%)
    pallas_call x1, Pallas kernels, body(): pl.pallas_call(functools.partial(kernel, dims), out_shape=[pltpu.VMEM((la...  69.6 us

profile of v5, /device:TPU:1, one launch (start us, length us, event | category | flops | bytes accessed | tf_op | source)
XLA Modules:
  0.0 71.3 jit_solution(15786767118223307633)
XLA Ops:
  0.6 69.6 %step.1 = (f32[64,768]{1,0:T(8,128)S(1)}, f32[64,768]{1,0:T(8,128)S(1)}, f32[64,768]{1,0:T(8,128)S(1)}, f32[192,768]{1,0:T(8,128)S(1)}, f32[12,384]{1,0:T(8,128)S(1)}, /*index=5*/f32[12,384]{1,0:T(8,128)S(1)}) custom-call(bf16[192,768]{1,0:T(8,128)(2,1)} %queries_h.1, s32[10,192]{1,0:T(8,128)} %bitcast.3, bf16[2048,768]{1,0:T(8,128)(2,1)} %bitcast.2, ...), custom_call_target="tpu_custom_call" | custom-call | flops 2415919104 | bytes 8388608 | tf_op jit(solution)/shard_map/step/pallas_call | solution.py:814
  70.2 1.1 %hand_over.1 = (f32[64,768]{1,0:T(8,128)}, f32[64,768]{1,0:T(8,128)}, f32[64,768]{1,0:T(8,128)}, f32[192,768]{1,0:T(8,128)}, f32[12,384]{1,0:T(8,128)}, /*index=5*/f32[12,384]{1,0:T(8,128)}) custom-call(f32[64,768]{1,0:T(8,128)S(1)} %get-tuple-element.12.refs_0_, f32[64,768]{1,0:T(8,128)S(1)} %get-tuple-element.13.refs_1_, ...), custom_call_target="tpu_custom_call" | custom-call | tf_op jit(solution)/shard_map/hand_over/pallas_call | solution.py:834
